TPU v7x, 32 devices: a whole 2x2x4 slice. The times are simulated.
32 devices in a mesh: dp: 4 (over y, x), seq: 8 (over z, core).
Axes of the slice: x: 2, y: 2, z: 4, core: 2. Of those that a mesh axis runs over, the one named last changes fastest.
Arguments:
- tokens: bfloat16 [4, 2048, 4096], P('dp', 'seq'), may hold values from -6 to 6
- w_qkv: bfloat16 [4096, 768], P('dp'), may hold values from -0.09375 to 0.09375
- norm_gain: float32 [256], replicated, may hold values from 0.1 to 1.9
- w_out: bfloat16 [256, 4096], P(None, 'dp'), may hold values from -0.375 to 0.375
Outputs:
- mixed: bfloat16 [4, 2048, 4096], P('dp', 'seq')
All inputs are finite; a program needn't handle non-finite values.
Results may differ from a plain program's by a relative error of at most 0.015.
Values may be sent and summed in bfloat16 or wider, within the bound.
No kernel may reach another device: no remote copies, remote signals or barrier semaphores. Data moves between devices by JAX's collectives and lax.ppermute only.
A program may use at most 64 MiB of HBM per device.

v0:
```python
import functools

import jax
import jax.numpy as jnp
from jax import lax
from jax.experimental import pallas as pl
from jax.experimental.pallas import tpu as pltpu
from jax.sharding import PartitionSpec as P

HEAD = 128
CORES = 2
VMEM_LIMIT = 24 * 1024 * 1024
CUT_LIMIT = 52 * 1024 * 1024
VMEM = pl.BlockSpec(memory_space=pltpu.VMEM)
HBM = pl.BlockSpec(memory_space=pltpu.HBM)


def flip(x, axis, size, mask):
    return lax.ppermute(x, axis, [(i, i ^ mask) for i in range(size)])


def dot(a, b, contract=((1,), (0,))):
    return lax.dot_general(a, b, (contract, ((), ())), preferred_element_type=jnp.float32)


def position():
    return lax.axis_index("dp"), lax.rem(lax.axis_index("seq"), CORES)


def quarter_of():
    return lax.rem(lax.axis_index("seq") // CORES, 4)


def cut_qkv(layout, w_qkv, *refs):
    outs, sem = refs[:-1], refs[-1]
    _, core = position()
    shard = w_qkv.shape[0]
    feat = w_qkv.shape[1] // 3
    copies = []
    for out, start in zip(outs, layout(shard)):
        rows = pl.ds(pl.multiple_of(start, 16), out.shape[0])
        for j in range(3):
            cols = pl.ds(pl.multiple_of(j * feat + core * HEAD, HEAD), HEAD)
            target = out.at[:, j * HEAD : (j + 1) * HEAD]
            copies.append(pltpu.make_async_copy(w_qkv.at[rows, cols], target, sem.at[len(copies)]))
            copies[-1].start()
    for copy in copies:
        copy.wait()


def cut_out(w_out, mine, theirs):
    _, core = position()
    for out, head in ((mine, core), (theirs, 1 - core)):
        out[...] = w_out[pl.ds(pl.multiple_of(head * HEAD, HEAD), HEAD), :]


def product(tok_a, tok_b, pieces, places):
    cols = [
        pl.ds(pl.multiple_of(place, 128), piece.shape[0]) for piece, place in zip(pieces, places)
    ]
    tok = jnp.concatenate(
        [jnp.concatenate([ref[:, c] for c in cols], axis=1) for ref in (tok_a, tok_b)], axis=0
    )
    weights = jnp.concatenate([piece[...] for piece in pieces], axis=0)
    return dot(tok, weights)


def places_near(shard, offsets):
    at = lax.axis_index("dp")
    return [(at ^ offset) * shard for offset in offsets]


def places_far(shard):
    start = places_near(shard, (3,))[0]
    mine = quarter_of()
    return [start + (mine ^ mask) * (shard // 4) for mask in (0, 2, 1, 3)]


def project(count, places, tok_a, tok_b, *refs):
    pieces, before, total = refs[:count], refs[count:-1], refs[-1]
    term = product(tok_a, tok_b, pieces, places())
    total[...] = before[0][...] + term if before else term


def project_states(count, places, tok_a, tok_b, *refs):
    pieces, before = refs[:count], refs[count:-4]
    act_out, value_out, state_out, chip_out = refs[-4:]
    proj = product(tok_a, tok_b, pieces, places())
    if before:
        proj = before[0][...] + proj
    rows = value_out.shape[1]
    chip = None
    for b in range(CORES):
        part = proj[b * rows : (b + 1) * rows, :]
        act = part[:, : 2 * HEAD]
        act = (act / (1.0 + jnp.exp(-act))).astype(jnp.bfloat16)
        values = part[:, 2 * HEAD :].astype(jnp.bfloat16)
        state = dot(act[:, HEAD:], values, ((0,), (0,)))
        chip = state if chip is None else chip + state
        act_out[b] = act
        value_out[b] = values
        state_out[b] = state
    chip_out[...] = chip.astype(jnp.bfloat16)


def attend(act, values, intra_out):
    rows = intra_out.shape[1]
    row = lax.broadcasted_iota(jnp.int32, (rows, rows), 0)
    col = lax.broadcasted_iota(jnp.int32, (rows, rows), 1)
    for b in range(CORES):
        scores = dot(act[b, :, :HEAD], act[b, :, HEAD:], ((1,), (1,)))
        scores = jnp.where(row >= col, scores, 0.0).astype(jnp.bfloat16)
        intra_out[b] = dot(scores, values[b])


def normalise(steps, act, state, intra, gain, *refs):
    got, (own_out, other_out) = refs[:steps], refs[steps:]
    _, core = position()
    chip_at = lax.axis_index("seq") // CORES
    base = jnp.zeros((HEAD, HEAD), jnp.float32)
    for step, ref in enumerate(got):
        base = base + jnp.where((chip_at >> step) % 2 == 1, ref[...].astype(jnp.float32), 0.0)
    odd = core == 1
    own_prefix = jnp.where(odd, base + state[1], base)
    other_prefix = jnp.where(odd, base, base + state[0])
    scale = gain[pl.ds(core, 1), :]
    for b, (prefix, out) in enumerate(((own_prefix, own_out), (other_prefix, other_out))):
        attended = dot(act[b, :, :HEAD], prefix.astype(jnp.bfloat16)) + intra[b]
        meansq = jnp.mean(attended * attended, axis=-1, keepdims=True)
        out[...] = (attended * lax.rsqrt(meansq + 1e-06) * scale).astype(jnp.bfloat16)


def mix(count, places, own, other, *refs):
    mine, theirs, (out, stage, sem) = refs[:count], refs[count : 2 * count], refs[2 * count :]
    normed = jnp.concatenate([own[...], other[...]], axis=1)
    copies = []
    slot = 0
    for my_rows, their_rows, place in zip(mine, theirs, places()):
        width = my_rows.shape[1]
        step = min(width, 512)
        for at_col in range(0, width, step):
            part = slice(at_col, at_col + step)
            weights = jnp.concatenate([my_rows[:, part], their_rows[:, part]], axis=0)
            here = stage.at[:, slot : slot + step]
            here[...] = dot(normed, weights).astype(jnp.bfloat16)
            cols = pl.ds(pl.multiple_of(place + at_col, 128), step)
            copies.append(pltpu.make_async_copy(here, out.at[:, cols], sem.at[len(copies)]))
            copies[-1].start()
            slot += step
    for copy in copies:
        copy.wait()


def places_out(width):
    at = lax.axis_index("dp")
    return [(at ^ offset) * width for offset in range(4)]


def shards(n, blocks, tokens, w_qkv, norm_gain, w_out):
    tok_own = tokens[0]
    rows, depth = tok_own.shape
    shard = w_qkv.shape[0]
    heads = norm_gain.shape[0] // HEAD
    bf16, f32 = jnp.bfloat16, jnp.float32

    def call(kernel, outs, ins, out_specs, in_specs, scratch=(), flops=0, moved=0, limit=VMEM_LIMIT):
        return pl.pallas_call(
            kernel,
            out_shape=outs,
            in_specs=in_specs,
            out_specs=out_specs,
            scratch_shapes=scratch,
            compiler_params=pltpu.CompilerParams(vmem_limit_bytes=limit),
            cost_estimate=pl.CostEstimate(flops=flops, bytes_accessed=moved, transcendentals=0),
        )(*ins)

    def array(shape, kind):
        return jax.ShapeDtypeStruct(shape, kind)

    def add_product(pieces, places, total=None):
        extra = [] if total is None else [total]
        return call(
            functools.partial(project, len(pieces), places),
            array((CORES * rows, 3 * HEAD), f32),
            [tok_own, tok_other, *pieces, *extra],
            VMEM, [VMEM] * (2 + len(pieces) + len(extra)),
            flops=rows * HEAD * (1 if total is not None else 1000000),
        )

    tok_other = flip(tok_own, "seq", blocks, 1)
    width = w_out.shape[1]
    grid = n == 4 and blocks % (4 * CORES) == 0 and shard % 512 == 0 and width % 256 == 0

    def cut(layout, *sizes):
        return call(
            functools.partial(cut_qkv, layout),
            [array((size, 3 * HEAD), bf16) for size in sizes],
            [w_qkv], [VMEM] * len(sizes), [HBM],
            scratch=[pltpu.SemaphoreType.DMA((3 * len(sizes),))], limit=CUT_LIMIT,
        )

    out_cut = functools.partial(
        call, cut_out, [array((HEAD, width), bf16)] * 2, [w_out], [VMEM] * 2, [VMEM]
    )
    total = None
    if grid:
        quarter = shard // 4
        own, part = cut(lambda shard: [0, quarter_of() * quarter], shard, quarter)
        far = [flip(part, "dp", n, 3)]
        from_x = flip(own, "dp", n, 1)
        from_y = flip(own, "dp", n, 2)
        far.append(flip(far[0], "seq", blocks, CORES * 2))
        far.append(flip(far[0], "seq", blocks, CORES))
        here, own = lax.optimization_barrier((far[0], own))
        total = add_product([own], functools.partial(places_near, shard, (0,)))
        passed, total = lax.optimization_barrier((far[1], total))
        far.append(flip(passed, "seq", blocks, CORES))
        own_mine, own_theirs = out_cut()
        sent = own_mine
        outs = []
        for i, mask in ((0, 1), (1, 2), (1, 3)):
            if mask == 1:
                sent, total = lax.optimization_barrier((sent, total))
            sent, far[1 + i] = lax.optimization_barrier((sent, far[1 + i]))
            outs.append(flip(sent, "dp", n, mask))
        out_x, out_y, out_d = outs
        total = add_product([from_x, from_y], functools.partial(places_near, shard, (1, 2)), total)
        pieces, places = far, functools.partial(places_far, shard)
    else:
        whole = cut(lambda shard: [0], shard)[0]
        pieces, places = [lax.all_gather(whole, "dp", axis=0, tiled=True)], lambda: [0]
    extra = [] if total is None else [total]

    act, values, state, chip = call(
        functools.partial(project_states, len(pieces), places),
        [
            array((CORES, rows, 2 * HEAD), bf16),
            array((CORES, rows, HEAD), bf16),
            array((CORES, HEAD, HEAD), f32),
            array((HEAD, HEAD), bf16),
        ],
        [tok_own, tok_other, *pieces, *extra],
        [VMEM] * 4, [VMEM] * (2 + len(pieces) + len(extra)),
        flops=2 * CORES * rows * sum(piece.shape[0] for piece in pieces) * 3 * HEAD,
    )
    intra = call(
        attend, array((CORES, rows, HEAD), f32), [act, values], VMEM, [VMEM] * 2,
        flops=4 * CORES * rows * rows * HEAD,
    )

    got, group = [], chip
    for step in range((blocks // CORES).bit_length() - 1):
        if got:
            group = (group.astype(f32) + got[-1].astype(f32)).astype(bf16)
            if grid:
                group, out_x, out_y = lax.optimization_barrier((group, out_x, out_y))
        got.append(flip(group, "seq", blocks, CORES << step))
    if grid:
        their_x = flip(out_x, "seq", blocks, 1)
        their_y = flip(out_y, "seq", blocks, 1)
    normed_own, normed_other = call(
        functools.partial(normalise, len(got)),
        [array((rows, HEAD), bf16)] * 2,
        [act, state, intra, norm_gain.reshape(heads, HEAD), *got],
        [VMEM] * 2, [VMEM] * (4 + len(got)),
    )
    normed_got = flip(normed_other, "seq", blocks, 1)

    if grid:
        out_d, normed_other = lax.optimization_barrier((out_d, normed_other))
        their_d = flip(out_d, "seq", blocks, 1)
        mine = [own_mine, out_x, out_y, out_d]
        theirs = [own_theirs, their_x, their_y, their_d]
        places = functools.partial(places_out, width)
    else:
        mine = [lax.all_gather(out_cut()[0], "dp", axis=1, tiled=True)]
        theirs = [flip(mine[0], "seq", blocks, 1)]
        places = lambda: [0]
    mixed = call(
        functools.partial(mix, len(mine), places),
        array((rows, n * width), bf16),
        [normed_own, normed_got, *mine, *theirs],
        HBM, [VMEM] * (2 + 2 * len(mine)),
        scratch=[pltpu.VMEM((rows, n * width), bf16), pltpu.SemaphoreType.DMA((16,))],
        flops=2 * rows * 2 * HEAD * n * width, moved=2 * rows * n * width,
    )
    return mixed[None]


def solution(mesh):
    n, blocks = mesh.shape["dp"], mesh.shape["seq"]
    return jax.shard_map(
        functools.partial(shards, n, blocks),
        mesh=mesh,
        in_specs=(P("dp", "seq", None), P("dp", None), P(), P(None, "dp")),
        out_specs=P("dp", "seq", None),
        check_vma=False,
    )
```

profile of v0, /device:TPU:0, one launch (start us, length us, event | category | flops | bytes accessed | tf_op | source)
XLA Modules:
  0.0 43.9 jit_solution(17076887004600988100)
XLA Ops:
  0.0 0.5 %collective-permute-start = (bf16[256,4096]{1,0:T(8,128)(2,1)}, bf16[256,4096]{1,0:T(8,128)(2,1)S(1)}, u32[]{:S(2)}, u32[]{:S(2)}) collective-permute-start(bf16[256,4096]{1,0:T(8,128)(2,1)} %bitcast.3), channel_id=1, source_target_pairs={{0,1},{1,0},{2,3},{3,2},{4,5},{5,4},{6,7},{7,6},{8,9},{9,8},{10,11... | collective-permute-start | bytes 6291464 | tf_op jit(solution)/shard_map/ppermute | solution.py:19
  0.5 1.3 %shard_map.46 = (bf16[1024,384]{1,0:T(8,128)(2,1)S(1)}, bf16[256,384]{1,0:T(8,128)(2,1)S(1)}) custom-call(bf16[1024,768]{1,0:T(8,128)(2,1)} %w_qkv.1), custom_call_target="tpu_custom_call" | custom-call | tf_op jit(solution)/shard_map/pallas_call | solution.py:167
  1.7 3.5 %collective-permute-start.1 = (bf16[256,384]{1,0:T(8,128)(2,1)S(1)}, bf16[256,384]{1,0:T(8,128)(2,1)S(1)}, u32[]{:S(2)}, u32[]{:S(2)}) collective-permute-start(bf16[256,384]{1,0:T(8,128)(2,1)S(1)} %get-tuple-element.29), channel_id=1, source_target_pairs={{0,24},{8,16},{16,8},{24,0},{1,25},{9,17},{17,9},{25,1},{2,26},{10... | collective-permute-start | bytes 589832 | tf_op jit(solution)/shard_map/ppermute | solution.py:19
  5.3 0.5 %collective-permute-start.5 = (bf16[1024,384]{1,0:T(8,128)(2,1)S(1)}, bf16[1024,384]{1,0:T(8,128)(2,1)S(1)}, u32[]{:S(2)}, u32[]{:S(2)}) collective-permute-start(bf16[1024,384]{1,0:T(8,128)(2,1)S(1)} %get-tuple-element.32.refs_0_), channel_id=1, source_target_pairs={{0,8},{8,0},{16,24},{24,16},{1,9},{9,1},{17,25},{25,17},{2,10},{10... | collective-permute-start | bytes 2359304 | tf_op jit(solution)/shard_map/ppermute | solution.py:19
  5.8 0.1 collective-permute-start.6
  5.9 5.2 %collective-permute-done.1.refs_0_ = bf16[256,384]{1,0:T(8,128)(2,1)S(1)} collective-permute-done((bf16[256,384]{1,0:T(8,128)(2,1)S(1)}, bf16[256,384]{1,0:T(8,128)(2,1)S(1)}, u32[]{:S(2)}, u32[]{:S(2)}) %collective-permute-start.1) | collective-permute-done | bytes 196640 | tf_op jit(solution)/shard_map/ppermute | solution.py:19
  11.1 3.0 %collective-permute-start.2 = (bf16[256,384]{1,0:T(8,128)(2,1)S(1)}, bf16[256,384]{1,0:T(8,128)(2,1)S(1)}, u32[]{:S(2)}, u32[]{:S(2)}) collective-permute-start(bf16[256,384]{1,0:T(8,128)(2,1)S(1)} %collective-permute-done.1.refs_0_), channel_id=1, source_target_pairs={{0,4},{1,5},{2,6},{3,7},{4,0},{5,1},{6,2},{7,3},{8,12},{9,13},{10,... | collective-permute-start | bytes 589832 | tf_op jit(solution)/shard_map/ppermute | solution.py:19
  14.0 1.6 %collective-permute-start.3 = (bf16[256,384]{1,0:T(8,128)(2,1)S(1)}, bf16[256,384]{1,0:T(8,128)(2,1)S(1)}, u32[]{:S(2)}, u32[]{:S(2)}) collective-permute-start(bf16[256,384]{1,0:T(8,128)(2,1)S(1)} %collective-permute-done.1.refs_0_), channel_id=1, source_target_pairs={{0,2},{1,3},{2,0},{3,1},{4,6},{5,7},{6,4},{7,5},{8,10},{9,11},{10,... | collective-permute-start | bytes 589832 | tf_op jit(solution)/shard_map/ppermute | solution.py:19
  15.6 1.6 %copy-done = bf16[1,256,4096]{2,1,0:T(8,128)(2,1)S(1)} copy-done((bf16[1,256,4096]{2,1,0:T(8,128)(2,1)S(1)}, bf16[1,256,4096]{2,1,0:T(8,128)(2,1)}, u32[]{:S(2)}) %copy-start) | copy-done | bytes 2097176
  17.2 0.7 %shard_map.48.refs_2_ = f32[512,384]{1,0:T(8,128)S(1)} custom-call(bf16[256,4096]{1,0:T(8,128)(2,1)S(1)} %bitcast.4, bf16[256,4096]{1,0:T(8,128)(2,1)S(1)} %collective-permute-done.tok_b, bf16[1024,384]{1,0:T(8,128)(2,1)S(1)} %get-tuple-element.32.refs_0_), custom_call_target="tpu_custom_call" | custom-call | flops 32768000000 | tf_op jit(solution)/shard_map/pallas_call | solution.py:167
  17.9 4.9 %collective-permute-done.2.refs_1_ = bf16[256,384]{1,0:T(8,128)(2,1)S(1)} collective-permute-done((bf16[256,384]{1,0:T(8,128)(2,1)S(1)}, bf16[256,384]{1,0:T(8,128)(2,1)S(1)}, u32[]{:S(2)}, u32[]{:S(2)}) %collective-permute-start.2) | collective-permute-done | bytes 196640 | tf_op jit(solution)/shard_map/ppermute | solution.py:19
  22.8 0.6 %collective-permute-start.4 = (bf16[256,384]{1,0:T(8,128)(2,1)S(1)}, bf16[256,384]{1,0:T(8,128)(2,1)S(1)}, u32[]{:S(2)}, u32[]{:S(2)}) collective-permute-start(bf16[256,384]{1,0:T(8,128)(2,1)S(1)} %collective-permute-done.2.refs_1_), channel_id=1, source_target_pairs={{0,2},{1,3},{2,0},{3,1},{4,6},{5,7},{6,4},{7,5},{8,10},{9,11},{10,... | collective-permute-start | bytes 589832 | tf_op jit(solution)/shard_map/ppermute | solution.py:19
  23.4 1.6 %collective-permute-start.8 = (bf16[128,1024]{1,0:T(8,128)(2,1)S(1)}, bf16[128,1024]{1,0:T(8,128)(2,1)S(1)}, u32[]{:S(2)}, u32[]{:S(2)}) collective-permute-start(bf16[128,1024]{1,0:T(8,128)(2,1)S(1)} %get-tuple-element.50.refs_0_), channel_id=1, source_target_pairs={{0,8},{8,0},{16,24},{24,16},{1,9},{9,1},{17,25},{25,17},{2,10},{10... | collective-permute-start | bytes 786440 | tf_op jit(solution)/shard_map/ppermute | solution.py:19
  24.9 1.5 %collective-permute-start.9 = (bf16[128,1024]{1,0:T(8,128)(2,1)S(1)}, bf16[128,1024]{1,0:T(8,128)(2,1)S(1)}, u32[]{:S(2)}, u32[]{:S(2)}) collective-permute-start(bf16[128,1024]{1,0:T(8,128)(2,1)S(1)} %get-tuple-element.50.refs_0_), channel_id=1, source_target_pairs={{0,16},{8,24},{16,0},{24,8},{1,17},{9,25},{17,1},{25,9},{2,18},{10... | collective-permute-start | bytes 786440 | tf_op jit(solution)/shard_map/ppermute | solution.py:19
  26.5 1.9 %collective-permute-done.5.refs_0_ = bf16[1024,384]{1,0:T(8,128)(2,1)S(1)} collective-permute-done((bf16[1024,384]{1,0:T(8,128)(2,1)S(1)}, bf16[1024,384]{1,0:T(8,128)(2,1)S(1)}, u32[]{:S(2)}, u32[]{:S(2)}) %collective-permute-start.5) | collective-permute-done | bytes 786464 | tf_op jit(solution)/shard_map/ppermute | solution.py:19
  28.4 0.0 collective-permute-done.6.refs_1_
  28.4 1.3 %shard_map.49.refs_4_ = f32[512,384]{1,0:T(8,128)S(1)} custom-call(bf16[256,4096]{1,0:T(8,128)(2,1)S(1)} %bitcast.5, bf16[256,4096]{1,0:T(8,128)(2,1)S(1)} %collective-permute-done.tok_b, bf16[1024,384]{1,0:T(8,128)(2,1)S(1)} %collective-permute-done.5.refs_0_, bf16[1024,384]{1,0:T(8,128)(2,1)S(1)} %collective-permute-done.6.refs_1_, ...), custom_call_target="tpu_custom_call" | custom-call | flops 32768 | tf_op jit(solution)/shard_map/pallas_call | solution.py:167
  29.6 0.0 copy-start.3
  29.7 1.0 %shard_map.50 = (bf16[2,256,256]{2,1,0:T(8,128)(2,1)S(1)}, bf16[2,256,128]{2,1,0:T(8,128)(2,1)S(1)}, f32[2,128,128]{2,1,0:T(8,128)S(1)}, bf16[128,128]{1,0:T(8,128)(2,1)S(1)}) custom-call(bf16[256,4096]{1,0:T(8,128)(2,1)S(1)} %bitcast.6, bf16[256,4096]{1,0:T(8,128)(2,1)S(1)} %collective-permute-done.tok_b, ...), custom_call_target="tpu_custom_call" | custom-call | flops 402653184 | tf_op jit(solution)/shard_map/pallas_call | solution.py:167
  30.6 1.6 %collective-permute-start.7 = (bf16[128,128]{1,0:T(8,128)(2,1)S(1)}, bf16[128,128]{1,0:T(8,128)(2,1)S(1)}, u32[]{:S(2)}, u32[]{:S(2)}) collective-permute-start(bf16[128,128]{1,0:T(8,128)(2,1)S(1)} %get-tuple-element.43), channel_id=1, source_target_pairs={{0,2},{1,3},{2,0},{3,1},{4,6},{5,7},{6,4},{7,5},{8,10},{9,11},{10,... | collective-permute-start | bytes 98312 | tf_op jit(solution)/shard_map/ppermute | solution.py:19
  32.3 2.0 %collective-permute-start.12 = (bf16[128,1024]{1,0:T(8,128)(2,1)S(1)}, bf16[128,1024]{1,0:T(8,128)(2,1)S(1)}, u32[]{:S(2)}, u32[]{:S(2)}) collective-permute-start(bf16[128,1024]{1,0:T(8,128)(2,1)S(1)} %get-tuple-element.50.refs_0_), channel_id=1, source_target_pairs={{0,24},{8,16},{16,8},{24,0},{1,25},{9,17},{17,9},{25,1},{2,26},{10... | collective-permute-start | bytes 786440 | tf_op jit(solution)/shard_map/ppermute | solution.py:19
  34.3 0.3 collective-permute-done.7.refs_0_
  34.6 2.6 %collective-permute-start.10 = (bf16[128,128]{1,0:T(8,128)(2,1)S(1)}, bf16[128,128]{1,0:T(8,128)(2,1)S(1)}, u32[]{:S(2)}, u32[]{:S(2)}) collective-permute-start(bf16[128,128]{1,0:T(8,128)(2,1)S(1)} %add_convert_fusion), channel_id=1, source_target_pairs={{0,4},{1,5},{2,6},{3,7},{4,0},{5,1},{6,2},{7,3},{8,12},{9,13},{10,... | collective-permute-start | bytes 98312 | tf_op jit(solution)/shard_map/ppermute | solution.py:19
  37.3 0.5 %shard_map.51.intra = f32[2,256,128]{2,1,0:T(8,128)S(1)} custom-call(bf16[2,256,256]{2,1,0:T(8,128)(2,1)S(1)} %get-tuple-element.40.act, bf16[2,256,128]{2,1,0:T(8,128)(2,1)S(1)} %get-tuple-element.42.values), custom_call_target="tpu_custom_call" | custom-call | flops 67108864 | tf_op jit(solution)/shard_map/pallas_call | solution.py:167
  37.8 0.1 collective-permute-start.13
  37.9 0.5 %collective-permute-start.14 = (bf16[128,1024]{1,0:T(8,128)(2,1)S(1)}, bf16[128,1024]{1,0:T(8,128)(2,1)S(1)}, u32[]{:S(2)}, u32[]{:S(2)}) collective-permute-start(bf16[128,1024]{1,0:T(8,128)(2,1)S(1)} %collective-permute-done.9.refs_2_), channel_id=1, source_target_pairs={{0,1},{1,0},{2,3},{3,2},{4,5},{5,4},{6,7},{7,6},{8,9},{9,8},{10,11... | collective-permute-start | bytes 786440 | tf_op jit(solution)/shard_map/ppermute | solution.py:19
  38.4 1.2 %collective-permute-done.10.refs_1_ = bf16[128,128]{1,0:T(8,128)(2,1)S(1)} collective-permute-done((bf16[128,128]{1,0:T(8,128)(2,1)S(1)}, bf16[128,128]{1,0:T(8,128)(2,1)S(1)}, u32[]{:S(2)}, u32[]{:S(2)}) %collective-permute-start.10) | collective-permute-done | bytes 32800 | tf_op jit(solution)/shard_map/ppermute | solution.py:19
  39.5 0.3 shard_map.52
  39.8 0.7 %collective-permute-done.12.refs_3_ = bf16[128,1024]{1,0:T(8,128)(2,1)S(1)} collective-permute-done((bf16[128,1024]{1,0:T(8,128)(2,1)S(1)}, bf16[128,1024]{1,0:T(8,128)(2,1)S(1)}, u32[]{:S(2)}, u32[]{:S(2)}) %collective-permute-start.12) | collective-permute-done | bytes 262176 | tf_op jit(solution)/shard_map/ppermute | solution.py:19
  40.6 0.5 %collective-permute-start.11 = (bf16[256,128]{1,0:T(8,128)(2,1)S(1)}, bf16[256,128]{1,0:T(8,128)(2,1)S(1)}, u32[]{:S(2)}, u32[]{:S(2)}) collective-permute-start(bf16[256,128]{1,0:T(8,128)(2,1)S(1)} %get-tuple-element.47), channel_id=1, source_target_pairs={{0,1},{1,0},{2,3},{3,2},{4,5},{5,4},{6,7},{7,6},{8,9},{9,8},{10,11... | collective-permute-start | bytes 196616 | tf_op jit(solution)/shard_map/ppermute | solution.py:19
  41.1 1.1 %collective-permute-done.11.other = bf16[256,128]{1,0:T(8,128)(2,1)S(1)} collective-permute-done((bf16[256,128]{1,0:T(8,128)(2,1)S(1)}, bf16[256,128]{1,0:T(8,128)(2,1)S(1)}, u32[]{:S(2)}, u32[]{:S(2)}) %collective-permute-start.11) | collective-permute-done | bytes 65568 | tf_op jit(solution)/shard_map/ppermute | solution.py:19
  42.2 1.7 %shard_map.53 = bf16[256,4096]{1,0:T(8,128)(2,1)} custom-call(bf16[256,128]{1,0:T(8,128)(2,1)S(1)} %get-tuple-element.46.own, bf16[256,128]{1,0:T(8,128)(2,1)S(1)} %collective-permute-done.11.other, bf16[128,1024]{1,0:T(8,128)(2,1)S(1)} %get-tuple-element.50.refs_0_, bf16[128,1024]{1,0:T(8,128)(2,1)S(1)} %collective-permute-done.8.refs_1_, ...), custom_call_target="tpu_custom_call" | custom-call | flops 536870912 | bytes 2097152 | tf_op jit(solution)/shard_map/pallas_call | solution.py:167
  (17 shorter events, 0.1 us)
Async XLA Ops:
  0.0 15.6 %collective-permute-start = (bf16[256,4096]{1,0:T(8,128)(2,1)}, bf16[256,4096]{1,0:T(8,128)(2,1)S(1)}, u32[]{:S(2)}, u32[]{:S(2)}) collective-permute-start(bf16[256,4096]{1,0:T(8,128)(2,1)} %bitcast.3), channel_id=1, source_target_pairs={{0,1},{1,0},{2,3},{3,2},{4,5},{5,4},{6,7},{7,6},{8,9},{9,8},{10,11... | collective-permute-start | bytes 6291464 | tf_op jit(solution)/shard_map/ppermute | solution.py:19
  0.5 22.9 %copy-start.2 = (bf16[256,1024]{1,0:T(8,128)(2,1)S(1)}, bf16[256,1024]{1,0:T(8,128)(2,1)}, u32[]{:S(2)}) copy-start(bf16[256,1024]{1,0:T(8,128)(2,1)} %w_out.1) | copy-start | bytes 1572868
  1.7 9.3 %collective-permute-start.1 = (bf16[256,384]{1,0:T(8,128)(2,1)S(1)}, bf16[256,384]{1,0:T(8,128)(2,1)S(1)}, u32[]{:S(2)}, u32[]{:S(2)}) collective-permute-start(bf16[256,384]{1,0:T(8,128)(2,1)S(1)} %get-tuple-element.29), channel_id=1, source_target_pairs={{0,24},{8,16},{16,8},{24,0},{1,25},{9,17},{17,9},{25,1},{2,26},{10... | collective-permute-start | bytes 589832 | tf_op jit(solution)/shard_map/ppermute | solution.py:19
  5.3 23.1 %collective-permute-start.5 = (bf16[1024,384]{1,0:T(8,128)(2,1)S(1)}, bf16[1024,384]{1,0:T(8,128)(2,1)S(1)}, u32[]{:S(2)}, u32[]{:S(2)}) collective-permute-start(bf16[1024,384]{1,0:T(8,128)(2,1)S(1)} %get-tuple-element.32.refs_0_), channel_id=1, source_target_pairs={{0,8},{8,0},{16,24},{24,16},{1,9},{9,1},{17,25},{25,17},{2,10},{10... | collective-permute-start | bytes 2359304 | tf_op jit(solution)/shard_map/ppermute | solution.py:19
  5.8 22.6 %collective-permute-start.6 = (bf16[1024,384]{1,0:T(8,128)(2,1)S(1)}, bf16[1024,384]{1,0:T(8,128)(2,1)S(1)}, u32[]{:S(2)}, u32[]{:S(2)}) collective-permute-start(bf16[1024,384]{1,0:T(8,128)(2,1)S(1)} %get-tuple-element.32.refs_0_), channel_id=1, source_target_pairs={{0,16},{8,24},{16,0},{24,8},{1,17},{9,25},{17,1},{25,9},{2,18},{10... | collective-permute-start | bytes 2359304 | tf_op jit(solution)/shard_map/ppermute | solution.py:19
  11.1 11.7 %collective-permute-start.2 = (bf16[256,384]{1,0:T(8,128)(2,1)S(1)}, bf16[256,384]{1,0:T(8,128)(2,1)S(1)}, u32[]{:S(2)}, u32[]{:S(2)}) collective-permute-start(bf16[256,384]{1,0:T(8,128)(2,1)S(1)} %collective-permute-done.1.refs_0_), channel_id=1, source_target_pairs={{0,4},{1,5},{2,6},{3,7},{4,0},{5,1},{6,2},{7,3},{8,12},{9,13},{10,... | collective-permute-start | bytes 589832 | tf_op jit(solution)/shard_map/ppermute | solution.py:19
  14.0 10.9 %collective-permute-start.3 = (bf16[256,384]{1,0:T(8,128)(2,1)S(1)}, bf16[256,384]{1,0:T(8,128)(2,1)S(1)}, u32[]{:S(2)}, u32[]{:S(2)}) collective-permute-start(bf16[256,384]{1,0:T(8,128)(2,1)S(1)} %collective-permute-done.1.refs_0_), channel_id=1, source_target_pairs={{0,2},{1,3},{2,0},{3,1},{4,6},{5,7},{6,4},{7,5},{8,10},{9,11},{10,... | collective-permute-start | bytes 589832 | tf_op jit(solution)/shard_map/ppermute | solution.py:19
  15.6 1.6 %copy-start = (bf16[1,256,4096]{2,1,0:T(8,128)(2,1)S(1)}, bf16[1,256,4096]{2,1,0:T(8,128)(2,1)}, u32[]{:S(2)}) copy-start(bf16[1,256,4096]{2,1,0:T(8,128)(2,1)} %param.4) | copy-start | bytes 6291460
  17.2 11.2 %copy-start.1 = (bf16[1,256,4096]{2,1,0:T(8,128)(2,1)S(1)}, bf16[1,256,4096]{2,1,0:T(8,128)(2,1)}, u32[]{:S(2)}) copy-start(bf16[1,256,4096]{2,1,0:T(8,128)(2,1)} %param.4) | copy-start | bytes 6291460
  22.8 6.9 %collective-permute-start.4 = (bf16[256,384]{1,0:T(8,128)(2,1)S(1)}, bf16[256,384]{1,0:T(8,128)(2,1)S(1)}, u32[]{:S(2)}, u32[]{:S(2)}) collective-permute-start(bf16[256,384]{1,0:T(8,128)(2,1)S(1)} %collective-permute-done.2.refs_1_), channel_id=1, source_target_pairs={{0,2},{1,3},{2,0},{3,1},{4,6},{5,7},{6,4},{7,5},{8,10},{9,11},{10,... | collective-permute-start | bytes 589832 | tf_op jit(solution)/shard_map/ppermute | solution.py:19
  23.4 11.2 %collective-permute-start.8 = (bf16[128,1024]{1,0:T(8,128)(2,1)S(1)}, bf16[128,1024]{1,0:T(8,128)(2,1)S(1)}, u32[]{:S(2)}, u32[]{:S(2)}) collective-permute-start(bf16[128,1024]{1,0:T(8,128)(2,1)S(1)} %get-tuple-element.50.refs_0_), channel_id=1, source_target_pairs={{0,8},{8,0},{16,24},{24,16},{1,9},{9,1},{17,25},{25,17},{2,10},{10... | collective-permute-start | bytes 786440 | tf_op jit(solution)/shard_map/ppermute | solution.py:19
  24.9 9.7 %collective-permute-start.9 = (bf16[128,1024]{1,0:T(8,128)(2,1)S(1)}, bf16[128,1024]{1,0:T(8,128)(2,1)S(1)}, u32[]{:S(2)}, u32[]{:S(2)}) collective-permute-start(bf16[128,1024]{1,0:T(8,128)(2,1)S(1)} %get-tuple-element.50.refs_0_), channel_id=1, source_target_pairs={{0,16},{8,24},{16,0},{24,8},{1,17},{9,25},{17,1},{25,9},{2,18},{10... | collective-permute-start | bytes 786440 | tf_op jit(solution)/shard_map/ppermute | solution.py:19
  29.6 9.9 %copy-start.3 = (f32[256]{0:T(256)S(1)}, f32[256]{0:T(256)}, u32[]{:S(2)}) copy-start(f32[256]{0:T(256)} %param.6) | copy-start | bytes 3076
  30.6 4.0 %collective-permute-start.7 = (bf16[128,128]{1,0:T(8,128)(2,1)S(1)}, bf16[128,128]{1,0:T(8,128)(2,1)S(1)}, u32[]{:S(2)}, u32[]{:S(2)}) collective-permute-start(bf16[128,128]{1,0:T(8,128)(2,1)S(1)} %get-tuple-element.43), channel_id=1, source_target_pairs={{0,2},{1,3},{2,0},{3,1},{4,6},{5,7},{6,4},{7,5},{8,10},{9,11},{10,... | collective-permute-start | bytes 98312 | tf_op jit(solution)/shard_map/ppermute | solution.py:19
  32.3 8.3 %collective-permute-start.12 = (bf16[128,1024]{1,0:T(8,128)(2,1)S(1)}, bf16[128,1024]{1,0:T(8,128)(2,1)S(1)}, u32[]{:S(2)}, u32[]{:S(2)}) collective-permute-start(bf16[128,1024]{1,0:T(8,128)(2,1)S(1)} %get-tuple-element.50.refs_0_), channel_id=1, source_target_pairs={{0,24},{8,16},{16,8},{24,0},{1,25},{9,17},{17,9},{25,1},{2,26},{10... | collective-permute-start | bytes 786440 | tf_op jit(solution)/shard_map/ppermute | solution.py:19
  34.6 4.9 %collective-permute-start.10 = (bf16[128,128]{1,0:T(8,128)(2,1)S(1)}, bf16[128,128]{1,0:T(8,128)(2,1)S(1)}, u32[]{:S(2)}, u32[]{:S(2)}) collective-permute-start(bf16[128,128]{1,0:T(8,128)(2,1)S(1)} %add_convert_fusion), channel_id=1, source_target_pairs={{0,4},{1,5},{2,6},{3,7},{4,0},{5,1},{6,2},{7,3},{8,12},{9,13},{10,... | collective-permute-start | bytes 98312 | tf_op jit(solution)/shard_map/ppermute | solution.py:19
  37.8 4.4 %collective-permute-start.13 = (bf16[128,1024]{1,0:T(8,128)(2,1)S(1)}, bf16[128,1024]{1,0:T(8,128)(2,1)S(1)}, u32[]{:S(2)}, u32[]{:S(2)}) collective-permute-start(bf16[128,1024]{1,0:T(8,128)(2,1)S(1)} %collective-permute-done.8.refs_1_), channel_id=1, source_target_pairs={{0,1},{1,0},{2,3},{3,2},{4,5},{5,4},{6,7},{7,6},{8,9},{9,8},{10,11... | collective-permute-start | bytes 786440 | tf_op jit(solution)/shard_map/ppermute | solution.py:19
  37.9 4.4 %collective-permute-start.14 = (bf16[128,1024]{1,0:T(8,128)(2,1)S(1)}, bf16[128,1024]{1,0:T(8,128)(2,1)S(1)}, u32[]{:S(2)}, u32[]{:S(2)}) collective-permute-start(bf16[128,1024]{1,0:T(8,128)(2,1)S(1)} %collective-permute-done.9.refs_2_), channel_id=1, source_target_pairs={{0,1},{1,0},{2,3},{3,2},{4,5},{5,4},{6,7},{7,6},{8,9},{9,8},{10,11... | collective-permute-start | bytes 786440 | tf_op jit(solution)/shard_map/ppermute | solution.py:19
  40.6 1.6 %collective-permute-start.15 = (bf16[128,1024]{1,0:T(8,128)(2,1)S(1)}, bf16[128,1024]{1,0:T(8,128)(2,1)S(1)}, u32[]{:S(2)}, u32[]{:S(2)}) collective-permute-start(bf16[128,1024]{1,0:T(8,128)(2,1)S(1)} %collective-permute-done.12.refs_3_), channel_id=1, source_target_pairs={{0,1},{1,0},{2,3},{3,2},{4,5},{5,4},{6,7},{7,6},{8,9},{9,8},{10,11... | collective-permute-start | bytes 786440 | tf_op jit(solution)/shard_map/ppermute | solution.py:19
  40.6 1.6 %collective-permute-start.11 = (bf16[256,128]{1,0:T(8,128)(2,1)S(1)}, bf16[256,128]{1,0:T(8,128)(2,1)S(1)}, u32[]{:S(2)}, u32[]{:S(2)}) collective-permute-start(bf16[256,128]{1,0:T(8,128)(2,1)S(1)} %get-tuple-element.47), channel_id=1, source_target_pairs={{0,1},{1,0},{2,3},{3,2},{4,5},{5,4},{6,7},{7,6},{8,9},{9,8},{10,11... | collective-permute-start | bytes 196616 | tf_op jit(solution)/shard_map/ppermute | solution.py:19
where the time goes:
time: 44.1 us; the launch traced here: 43.9 us
  starting transfers between devices  20.1 us (46%)
  waiting for transfers between devices  15.3 us (35%)
  Pallas kernels  6.75 us (15%)
  local copies, waits for them, and re-layouts  1.61 us (4%)
    ppermute x16, starting transfers between devices, flip(): return lax.ppermute(x, axis, [(i, i ^ mask) for i in range(size)])  20.1 us
    ppermute x16, waiting for transfers between devices, flip(): return lax.ppermute(x, axis, [(i, i ^ mask) for i in range(size)])  15.3 us
    pallas_call x8, Pallas kernels, call(): pl.pallas_call(kernel, out_shape=outs, in_specs=in_specs, out_specs=out_s...  6.75 us
    unnamed x8, local copies, waits for them, and re-layouts  1.61 us
  transfers between devices with their start and end apart: 16, of which 7 were waited for; matrix products, arithmetic and copies ran while one was open for 0% of the time, Pallas kernels for 12%

commit v1 on v0

--- a/solution.py
+++ b/solution.py
@@ -217,15 +217,14 @@
         far.append(flip(passed, "seq", blocks, CORES))
         own_mine, own_theirs = out_cut()
         sent = own_mine
-        outs = []
-        for i, mask in ((0, 1), (1, 2), (1, 3)):
-            if mask == 1:
-                sent, total = lax.optimization_barrier((sent, total))
-            sent, far[1 + i] = lax.optimization_barrier((sent, far[1 + i]))
-            outs.append(flip(sent, "dp", n, mask))
-        out_x, out_y, out_d = outs
+        sent, total, far[1] = lax.optimization_barrier((sent, total, far[1]))
+        out_d = flip(sent, "dp", n, 3)
+        total = add_product(far[:3], lambda: places_far(shard)[:3], total)
+        sent, total = lax.optimization_barrier((sent, total))
+        out_x = flip(sent, "dp", n, 1)
+        out_y = flip(sent, "dp", n, 2)
         total = add_product([from_x, from_y], functools.partial(places_near, shard, (1, 2)), total)
-        pieces, places = far, functools.partial(places_far, shard)
+        pieces, places = far[3:], lambda: places_far(shard)[3:]
     else:
         whole = cut(lambda shard: [0], shard)[0]
         pieces, places = [lax.all_gather(whole, "dp", axis=0, tiled=True)], lambda: [0]
@@ -253,11 +252,10 @@
         if got:
             group = (group.astype(f32) + got[-1].astype(f32)).astype(bf16)
             if grid:
-                group, out_x, out_y = lax.optimization_barrier((group, out_x, out_y))
+                group, out_d = lax.optimization_barrier((group, out_d))
         got.append(flip(group, "seq", blocks, CORES << step))
     if grid:
-        their_x = flip(out_x, "seq", blocks, 1)
-        their_y = flip(out_y, "seq", blocks, 1)
+        their_d = flip(out_d, "seq", blocks, 1)
     normed_own, normed_other = call(
         functools.partial(normalise, len(got)),
         [array((rows, HEAD), bf16)] * 2,
@@ -267,8 +265,9 @@
     normed_got = flip(normed_other, "seq", blocks, 1)
 
     if grid:
-        out_d, normed_other = lax.optimization_barrier((out_d, normed_other))
-        their_d = flip(out_d, "seq", blocks, 1)
+        out_x, out_y, normed_other = lax.optimization_barrier((out_x, out_y, normed_other))
+        their_x = flip(out_x, "seq", blocks, 1)
+        their_y = flip(out_y, "seq", blocks, 1)
         mine = [own_mine, out_x, out_y, out_d]
         theirs = [own_theirs, their_x, their_y, their_d]
         places = functools.partial(places_out, width)

time: 44.1 us -> 44.6 us (1.011)
  waiting for transfers between devices: 15.3 us -> 15.9 us
    ppermute x16, waiting for transfers between devices: 15.3 us -> 15.9 us  [flip(): return lax.ppermute(x, axis, [(i, i ^ mask) for i in range(size)])]
    pallas_call x8 -> x9, Pallas kernels: 6.75 us -> 6.92 us  [call(): pl.pallas_call(kernel, out_shape=outs, in_specs=in_specs, out_specs=out_s...]
  transfers between devices with their start and end apart: 16 -> 16, of which waited for: 7 -> 6; matrix products, arithmetic and copies ran while one was open for 0% -> 0% of each run, Pallas kernels for 12% -> 12%
where the time goes in v1:
time: 44.6 us; the launch traced here: 44.5 us
  starting transfers between devices  19.9 us (45%)
  waiting for transfers between devices  15.9 us (36%)
  Pallas kernels  6.92 us (16%)
  local copies, waits for them, and re-layouts  1.61 us (4%)
    ppermute x16, starting transfers between devices, flip(): return lax.ppermute(x, axis, [(i, i ^ mask) for i in range(size)])  19.9 us
    ppermute x16, waiting for transfers between devices, flip(): return lax.ppermute(x, axis, [(i, i ^ mask) for i in range(size)])  15.9 us
    pallas_call x9, Pallas kernels, call(): pl.pallas_call(kernel, out_shape=outs, in_specs=in_specs, out_specs=out_s...  6.92 us
    unnamed x8, local copies, waits for them, and re-layouts  1.61 us
  transfers between devices with their start and end apart: 16, of which 6 were waited for; matrix products, arithmetic and copies ran while one was open for 0% of the time, Pallas kernels for 12%

profile of v1, /device:TPU:0, one launch (start us, length us, event | category | flops | bytes accessed | tf_op | source)
XLA Modules:
  0.0 44.5 jit_solution(4395010727940296778)
XLA Ops:
  0.0 0.5 %collective-permute-start = (bf16[256,4096]{1,0:T(8,128)(2,1)}, bf16[256,4096]{1,0:T(8,128)(2,1)S(1)}, u32[]{:S(2)}, u32[]{:S(2)}) collective-permute-start(bf16[256,4096]{1,0:T(8,128)(2,1)} %bitcast.3), channel_id=1, source_target_pairs={{0,1},{1,0},{2,3},{3,2},{4,5},{5,4},{6,7},{7,6},{8,9},{9,8},{10,11... | collective-permute-start | bytes 6291464 | tf_op jit(solution)/shard_map/ppermute | solution.py:19
  0.5 1.3 %shard_map.46 = (bf16[1024,384]{1,0:T(8,128)(2,1)S(1)}, bf16[256,384]{1,0:T(8,128)(2,1)S(1)}) custom-call(bf16[1024,768]{1,0:T(8,128)(2,1)} %w_qkv.1), custom_call_target="tpu_custom_call" | custom-call | tf_op jit(solution)/shard_map/pallas_call | solution.py:167
  1.7 3.5 %collective-permute-start.1 = (bf16[256,384]{1,0:T(8,128)(2,1)S(1)}, bf16[256,384]{1,0:T(8,128)(2,1)S(1)}, u32[]{:S(2)}, u32[]{:S(2)}) collective-permute-start(bf16[256,384]{1,0:T(8,128)(2,1)S(1)} %get-tuple-element.27), channel_id=1, source_target_pairs={{0,24},{8,16},{16,8},{24,0},{1,25},{9,17},{17,9},{25,1},{2,26},{10... | collective-permute-start | bytes 589832 | tf_op jit(solution)/shard_map/ppermute | solution.py:19
  5.3 0.5 %collective-permute-start.4 = (bf16[1024,384]{1,0:T(8,128)(2,1)S(1)}, bf16[1024,384]{1,0:T(8,128)(2,1)S(1)}, u32[]{:S(2)}, u32[]{:S(2)}) collective-permute-start(bf16[1024,384]{1,0:T(8,128)(2,1)S(1)} %get-tuple-element.29.refs_0_), channel_id=1, source_target_pairs={{0,8},{8,0},{16,24},{24,16},{1,9},{9,1},{17,25},{25,17},{2,10},{10... | collective-permute-start | bytes 2359304 | tf_op jit(solution)/shard_map/ppermute | solution.py:19
  5.8 0.1 collective-permute-start.5
  5.9 5.2 %collective-permute-done.1.refs_0_ = bf16[256,384]{1,0:T(8,128)(2,1)S(1)} collective-permute-done((bf16[256,384]{1,0:T(8,128)(2,1)S(1)}, bf16[256,384]{1,0:T(8,128)(2,1)S(1)}, u32[]{:S(2)}, u32[]{:S(2)}) %collective-permute-start.1) | collective-permute-done | bytes 196640 | tf_op jit(solution)/shard_map/ppermute | solution.py:19
  11.1 3.0 %collective-permute-start.2 = (bf16[256,384]{1,0:T(8,128)(2,1)S(1)}, bf16[256,384]{1,0:T(8,128)(2,1)S(1)}, u32[]{:S(2)}, u32[]{:S(2)}) collective-permute-start(bf16[256,384]{1,0:T(8,128)(2,1)S(1)} %collective-permute-done.1.refs_0_), channel_id=1, source_target_pairs={{0,4},{1,5},{2,6},{3,7},{4,0},{5,1},{6,2},{7,3},{8,12},{9,13},{10,... | collective-permute-start | bytes 589832 | tf_op jit(solution)/shard_map/ppermute | solution.py:19
  14.0 1.6 %collective-permute-start.6 = (bf16[256,384]{1,0:T(8,128)(2,1)S(1)}, bf16[256,384]{1,0:T(8,128)(2,1)S(1)}, u32[]{:S(2)}, u32[]{:S(2)}) collective-permute-start(bf16[256,384]{1,0:T(8,128)(2,1)S(1)} %collective-permute-done.1.refs_0_), channel_id=1, source_target_pairs={{0,2},{1,3},{2,0},{3,1},{4,6},{5,7},{6,4},{7,5},{8,10},{9,11},{10,... | collective-permute-start | bytes 589832 | tf_op jit(solution)/shard_map/ppermute | solution.py:19
  15.6 1.6 %copy-done = bf16[1,256,4096]{2,1,0:T(8,128)(2,1)S(1)} copy-done((bf16[1,256,4096]{2,1,0:T(8,128)(2,1)S(1)}, bf16[1,256,4096]{2,1,0:T(8,128)(2,1)}, u32[]{:S(2)}) %copy-start) | copy-done | bytes 2097176
  17.2 0.7 %shard_map.47.refs_3_ = f32[512,384]{1,0:T(8,128)S(1)} custom-call(bf16[256,4096]{1,0:T(8,128)(2,1)S(1)} %bitcast.4, bf16[256,4096]{1,0:T(8,128)(2,1)S(1)} %collective-permute-done.tok_b, bf16[1024,384]{1,0:T(8,128)(2,1)S(1)} %get-tuple-element.29.refs_0_), custom_call_target="tpu_custom_call" | custom-call | flops 32768000000 | tf_op jit(solution)/shard_map/pallas_call | solution.py:167
  17.9 4.9 %collective-permute-done.2.refs_1_ = bf16[256,384]{1,0:T(8,128)(2,1)S(1)} collective-permute-done((bf16[256,384]{1,0:T(8,128)(2,1)S(1)}, bf16[256,384]{1,0:T(8,128)(2,1)S(1)}, u32[]{:S(2)}, u32[]{:S(2)}) %collective-permute-start.2) | collective-permute-done | bytes 196640 | tf_op jit(solution)/shard_map/ppermute | solution.py:19
  22.8 0.6 %collective-permute-start.3 = (bf16[256,384]{1,0:T(8,128)(2,1)S(1)}, bf16[256,384]{1,0:T(8,128)(2,1)S(1)}, u32[]{:S(2)}, u32[]{:S(2)}) collective-permute-start(bf16[256,384]{1,0:T(8,128)(2,1)S(1)} %collective-permute-done.2.refs_1_), channel_id=1, source_target_pairs={{0,2},{1,3},{2,0},{3,1},{4,6},{5,7},{6,4},{7,5},{8,10},{9,11},{10,... | collective-permute-start | bytes 589832 | tf_op jit(solution)/shard_map/ppermute | solution.py:19
  23.4 2.5 %collective-permute-start.8 = (bf16[128,1024]{1,0:T(8,128)(2,1)S(1)}, bf16[128,1024]{1,0:T(8,128)(2,1)S(1)}, u32[]{:S(2)}, u32[]{:S(2)}) collective-permute-start(bf16[128,1024]{1,0:T(8,128)(2,1)S(1)} %get-tuple-element.44.refs_0_), channel_id=1, source_target_pairs={{0,24},{8,16},{16,8},{24,0},{1,25},{9,17},{17,9},{25,1},{2,26},{10... | collective-permute-start | bytes 786440 | tf_op jit(solution)/shard_map/ppermute | solution.py:19
  25.9 0.0 collective-permute-done.6.refs_2_
  25.9 0.6 %shard_map.49.refs_2_ = f32[512,384]{1,0:T(8,128)S(1)} custom-call(bf16[256,4096]{1,0:T(8,128)(2,1)S(1)} %bitcast.5, bf16[256,4096]{1,0:T(8,128)(2,1)S(1)} %collective-permute-done.tok_b, bf16[256,384]{1,0:T(8,128)(2,1)S(1)} %collective-permute-done.1.refs_0_, bf16[256,384]{1,0:T(8,128)(2,1)S(1)} %collective-permute-done.2.refs_1_, ...), custom_call_target="tpu_custom_call" | custom-call | flops 32768 | tf_op jit(solution)/shard_map/pallas_call | solution.py:167
  26.5 1.9 %collective-permute-done.4.refs_0_ = bf16[1024,384]{1,0:T(8,128)(2,1)S(1)} collective-permute-done((bf16[1024,384]{1,0:T(8,128)(2,1)S(1)}, bf16[1024,384]{1,0:T(8,128)(2,1)S(1)}, u32[]{:S(2)}, u32[]{:S(2)}) %collective-permute-start.4) | collective-permute-done | bytes 786464 | tf_op jit(solution)/shard_map/ppermute | solution.py:19
  28.4 1.3 %shard_map.50.refs_1_ = f32[512,384]{1,0:T(8,128)S(1)} custom-call(bf16[256,4096]{1,0:T(8,128)(2,1)S(1)} %bitcast.6, bf16[256,4096]{1,0:T(8,128)(2,1)S(1)} %collective-permute-done.tok_b, bf16[1024,384]{1,0:T(8,128)(2,1)S(1)} %collective-permute-done.4.refs_0_, bf16[1024,384]{1,0:T(8,128)(2,1)S(1)} %collective-permute-done.5.refs_1_, ...), custom_call_target="tpu_custom_call" | custom-call | flops 32768 | tf_op jit(solution)/shard_map/pallas_call | solution.py:167
  29.6 0.0 copy-start.3
  29.7 0.5 %shard_map.51 = (bf16[2,256,256]{2,1,0:T(8,128)(2,1)S(1)}, bf16[2,256,128]{2,1,0:T(8,128)(2,1)S(1)}, f32[2,128,128]{2,1,0:T(8,128)S(1)}, bf16[128,128]{1,0:T(8,128)(2,1)S(1)}) custom-call(bf16[256,4096]{1,0:T(8,128)(2,1)S(1)} %bitcast.7, bf16[256,4096]{1,0:T(8,128)(2,1)S(1)} %collective-permute-done.tok_b, ...), custom_call_target="tpu_custom_call" | custom-call | flops 100663296 | tf_op jit(solution)/shard_map/pallas_call | solution.py:167
  30.2 1.6 %collective-permute-start.7 = (bf16[128,128]{1,0:T(8,128)(2,1)S(1)}, bf16[128,128]{1,0:T(8,128)(2,1)S(1)}, u32[]{:S(2)}, u32[]{:S(2)}) collective-permute-start(bf16[128,128]{1,0:T(8,128)(2,1)S(1)} %get-tuple-element.40), channel_id=1, source_target_pairs={{0,2},{1,3},{2,0},{3,1},{4,6},{5,7},{6,4},{7,5},{8,10},{9,11},{10,... | collective-permute-start | bytes 98312 | tf_op jit(solution)/shard_map/ppermute | solution.py:19
  31.8 1.5 %collective-permute-start.11 = (bf16[128,1024]{1,0:T(8,128)(2,1)S(1)}, bf16[128,1024]{1,0:T(8,128)(2,1)S(1)}, u32[]{:S(2)}, u32[]{:S(2)}) collective-permute-start(bf16[128,1024]{1,0:T(8,128)(2,1)S(1)} %get-tuple-element.44.refs_0_), channel_id=1, source_target_pairs={{0,8},{8,0},{16,24},{24,16},{1,9},{9,1},{17,25},{25,17},{2,10},{10... | collective-permute-start | bytes 786440 | tf_op jit(solution)/shard_map/ppermute | solution.py:19
  33.3 1.4 %collective-permute-start.12 = (bf16[128,1024]{1,0:T(8,128)(2,1)S(1)}, bf16[128,1024]{1,0:T(8,128)(2,1)S(1)}, u32[]{:S(2)}, u32[]{:S(2)}) collective-permute-start(bf16[128,1024]{1,0:T(8,128)(2,1)S(1)} %get-tuple-element.44.refs_0_), channel_id=1, source_target_pairs={{0,16},{8,24},{16,0},{24,8},{1,17},{9,25},{17,1},{25,9},{2,18},{10... | collective-permute-start | bytes 786440 | tf_op jit(solution)/shard_map/ppermute | solution.py:19
  34.7 2.6 %collective-permute-start.9 = (bf16[128,128]{1,0:T(8,128)(2,1)S(1)}, bf16[128,128]{1,0:T(8,128)(2,1)S(1)}, u32[]{:S(2)}, u32[]{:S(2)}) collective-permute-start(bf16[128,128]{1,0:T(8,128)(2,1)S(1)} %add_convert_fusion), channel_id=1, source_target_pairs={{0,4},{1,5},{2,6},{3,7},{4,0},{5,1},{6,2},{7,3},{8,12},{9,13},{10,... | collective-permute-start | bytes 98312 | tf_op jit(solution)/shard_map/ppermute | solution.py:19
  37.4 0.5 %shard_map.52.intra = f32[2,256,128]{2,1,0:T(8,128)S(1)} custom-call(bf16[2,256,256]{2,1,0:T(8,128)(2,1)S(1)} %get-tuple-element.37.act, bf16[2,256,128]{2,1,0:T(8,128)(2,1)S(1)} %get-tuple-element.39.values), custom_call_target="tpu_custom_call" | custom-call | flops 67108864 | tf_op jit(solution)/shard_map/pallas_call | solution.py:167
  37.9 0.1 collective-permute-start.15
  38.0 1.6 %collective-permute-done.9.refs_1_ = bf16[128,128]{1,0:T(8,128)(2,1)S(1)} collective-permute-done((bf16[128,128]{1,0:T(8,128)(2,1)S(1)}, bf16[128,128]{1,0:T(8,128)(2,1)S(1)}, u32[]{:S(2)}, u32[]{:S(2)}) %collective-permute-start.9) | collective-permute-done | bytes 32800 | tf_op jit(solution)/shard_map/ppermute | solution.py:19
  39.6 0.3 shard_map.53
  39.9 0.8 %collective-permute-done.12.refs_2_ = bf16[128,1024]{1,0:T(8,128)(2,1)S(1)} collective-permute-done((bf16[128,1024]{1,0:T(8,128)(2,1)S(1)}, bf16[128,1024]{1,0:T(8,128)(2,1)S(1)}, u32[]{:S(2)}, u32[]{:S(2)}) %collective-permute-start.12) | collective-permute-done | bytes 262176 | tf_op jit(solution)/shard_map/ppermute | solution.py:19
  40.8 0.5 %collective-permute-start.14 = (bf16[128,1024]{1,0:T(8,128)(2,1)S(1)}, bf16[128,1024]{1,0:T(8,128)(2,1)S(1)}, u32[]{:S(2)}, u32[]{:S(2)}) collective-permute-start(bf16[128,1024]{1,0:T(8,128)(2,1)S(1)} %collective-permute-done.12.refs_2_), channel_id=1, source_target_pairs={{0,1},{1,0},{2,3},{3,2},{4,5},{5,4},{6,7},{7,6},{8,9},{9,8},{10,11... | collective-permute-start | bytes 786440 | tf_op jit(solution)/shard_map/ppermute | solution.py:19
  41.3 0.0 collective-permute-start.10
  41.3 1.5 %collective-permute-done.10.other = bf16[256,128]{1,0:T(8,128)(2,1)S(1)} collective-permute-done((bf16[256,128]{1,0:T(8,128)(2,1)S(1)}, bf16[256,128]{1,0:T(8,128)(2,1)S(1)}, u32[]{:S(2)}, u32[]{:S(2)}) %collective-permute-start.10) | collective-permute-done | bytes 65568 | tf_op jit(solution)/shard_map/ppermute | solution.py:19
  42.8 1.7 %shard_map.54 = bf16[256,4096]{1,0:T(8,128)(2,1)} custom-call(bf16[256,128]{1,0:T(8,128)(2,1)S(1)} %get-tuple-element.42.own, bf16[256,128]{1,0:T(8,128)(2,1)S(1)} %collective-permute-done.10.other, bf16[128,1024]{1,0:T(8,128)(2,1)S(1)} %get-tuple-element.44.refs_0_, bf16[128,1024]{1,0:T(8,128)(2,1)S(1)} %collective-permute-done.11.refs_1_, ...), custom_call_target="tpu_custom_call" | custom-call | flops 536870912 | bytes 2097152 | tf_op jit(solution)/shard_map/pallas_call | solution.py:167
  (18 shorter events, 0.1 us)
Async XLA Ops:
  0.0 15.6 %collective-permute-start = (bf16[256,4096]{1,0:T(8,128)(2,1)}, bf16[256,4096]{1,0:T(8,128)(2,1)S(1)}, u32[]{:S(2)}, u32[]{:S(2)}) collective-permute-start(bf16[256,4096]{1,0:T(8,128)(2,1)} %bitcast.3), channel_id=1, source_target_pairs={{0,1},{1,0},{2,3},{3,2},{4,5},{5,4},{6,7},{7,6},{8,9},{9,8},{10,11... | collective-permute-start | bytes 6291464 | tf_op jit(solution)/shard_map/ppermute | solution.py:19
  0.5 22.9 %copy-start.2 = (bf16[256,1024]{1,0:T(8,128)(2,1)S(1)}, bf16[256,1024]{1,0:T(8,128)(2,1)}, u32[]{:S(2)}) copy-start(bf16[256,1024]{1,0:T(8,128)(2,1)} %w_out.1) | copy-start | bytes 1572868
  1.7 9.3 %collective-permute-start.1 = (bf16[256,384]{1,0:T(8,128)(2,1)S(1)}, bf16[256,384]{1,0:T(8,128)(2,1)S(1)}, u32[]{:S(2)}, u32[]{:S(2)}) collective-permute-start(bf16[256,384]{1,0:T(8,128)(2,1)S(1)} %get-tuple-element.27), channel_id=1, source_target_pairs={{0,24},{8,16},{16,8},{24,0},{1,25},{9,17},{17,9},{25,1},{2,26},{10... | collective-permute-start | bytes 589832 | tf_op jit(solution)/shard_map/ppermute | solution.py:19
  5.3 23.1 %collective-permute-start.4 = (bf16[1024,384]{1,0:T(8,128)(2,1)S(1)}, bf16[1024,384]{1,0:T(8,128)(2,1)S(1)}, u32[]{:S(2)}, u32[]{:S(2)}) collective-permute-start(bf16[1024,384]{1,0:T(8,128)(2,1)S(1)} %get-tuple-element.29.refs_0_), channel_id=1, source_target_pairs={{0,8},{8,0},{16,24},{24,16},{1,9},{9,1},{17,25},{25,17},{2,10},{10... | collective-permute-start | bytes 2359304 | tf_op jit(solution)/shard_map/ppermute | solution.py:19
  5.8 22.6 %collective-permute-start.5 = (bf16[1024,384]{1,0:T(8,128)(2,1)S(1)}, bf16[1024,384]{1,0:T(8,128)(2,1)S(1)}, u32[]{:S(2)}, u32[]{:S(2)}) collective-permute-start(bf16[1024,384]{1,0:T(8,128)(2,1)S(1)} %get-tuple-element.29.refs_0_), channel_id=1, source_target_pairs={{0,16},{8,24},{16,0},{24,8},{1,17},{9,25},{17,1},{25,9},{2,18},{10... | collective-permute-start | bytes 2359304 | tf_op jit(solution)/shard_map/ppermute | solution.py:19
  11.1 11.7 %collective-permute-start.2 = (bf16[256,384]{1,0:T(8,128)(2,1)S(1)}, bf16[256,384]{1,0:T(8,128)(2,1)S(1)}, u32[]{:S(2)}, u32[]{:S(2)}) collective-permute-start(bf16[256,384]{1,0:T(8,128)(2,1)S(1)} %collective-permute-done.1.refs_0_), channel_id=1, source_target_pairs={{0,4},{1,5},{2,6},{3,7},{4,0},{5,1},{6,2},{7,3},{8,12},{9,13},{10,... | collective-permute-start | bytes 589832 | tf_op jit(solution)/shard_map/ppermute | solution.py:19
  14.0 11.9 %collective-permute-start.6 = (bf16[256,384]{1,0:T(8,128)(2,1)S(1)}, bf16[256,384]{1,0:T(8,128)(2,1)S(1)}, u32[]{:S(2)}, u32[]{:S(2)}) collective-permute-start(bf16[256,384]{1,0:T(8,128)(2,1)S(1)} %collective-permute-done.1.refs_0_), channel_id=1, source_target_pairs={{0,2},{1,3},{2,0},{3,1},{4,6},{5,7},{6,4},{7,5},{8,10},{9,11},{10,... | collective-permute-start | bytes 589832 | tf_op jit(solution)/shard_map/ppermute | solution.py:19
  15.6 1.6 %copy-start = (bf16[1,256,4096]{2,1,0:T(8,128)(2,1)S(1)}, bf16[1,256,4096]{2,1,0:T(8,128)(2,1)}, u32[]{:S(2)}) copy-start(bf16[1,256,4096]{2,1,0:T(8,128)(2,1)} %param.4) | copy-start | bytes 6291460
  17.2 8.7 %copy-start.1 = (bf16[1,256,4096]{2,1,0:T(8,128)(2,1)S(1)}, bf16[1,256,4096]{2,1,0:T(8,128)(2,1)}, u32[]{:S(2)}) copy-start(bf16[1,256,4096]{2,1,0:T(8,128)(2,1)} %param.4) | copy-start | bytes 6291460
  22.8 6.9 %collective-permute-start.3 = (bf16[256,384]{1,0:T(8,128)(2,1)S(1)}, bf16[256,384]{1,0:T(8,128)(2,1)S(1)}, u32[]{:S(2)}, u32[]{:S(2)}) collective-permute-start(bf16[256,384]{1,0:T(8,128)(2,1)S(1)} %collective-permute-done.2.refs_1_), channel_id=1, source_target_pairs={{0,2},{1,3},{2,0},{3,1},{4,6},{5,7},{6,4},{7,5},{8,10},{9,11},{10,... | collective-permute-start | bytes 589832 | tf_op jit(solution)/shard_map/ppermute | solution.py:19
  23.4 11.3 %collective-permute-start.8 = (bf16[128,1024]{1,0:T(8,128)(2,1)S(1)}, bf16[128,1024]{1,0:T(8,128)(2,1)S(1)}, u32[]{:S(2)}, u32[]{:S(2)}) collective-permute-start(bf16[128,1024]{1,0:T(8,128)(2,1)S(1)} %get-tuple-element.44.refs_0_), channel_id=1, source_target_pairs={{0,24},{8,16},{16,8},{24,0},{1,25},{9,17},{17,9},{25,1},{2,26},{10... | collective-permute-start | bytes 786440 | tf_op jit(solution)/shard_map/ppermute | solution.py:19
  29.6 10.0 %copy-start.3 = (f32[256]{0:T(256)S(1)}, f32[256]{0:T(256)}, u32[]{:S(2)}) copy-start(f32[256]{0:T(256)} %param.6) | copy-start | bytes 3076
  30.2 4.5 %collective-permute-start.7 = (bf16[128,128]{1,0:T(8,128)(2,1)S(1)}, bf16[128,128]{1,0:T(8,128)(2,1)S(1)}, u32[]{:S(2)}, u32[]{:S(2)}) collective-permute-start(bf16[128,128]{1,0:T(8,128)(2,1)S(1)} %get-tuple-element.40), channel_id=1, source_target_pairs={{0,2},{1,3},{2,0},{3,1},{4,6},{5,7},{6,4},{7,5},{8,10},{9,11},{10,... | collective-permute-start | bytes 98312 | tf_op jit(solution)/shard_map/ppermute | solution.py:19
  31.8 8.1 %collective-permute-start.11 = (bf16[128,1024]{1,0:T(8,128)(2,1)S(1)}, bf16[128,1024]{1,0:T(8,128)(2,1)S(1)}, u32[]{:S(2)}, u32[]{:S(2)}) collective-permute-start(bf16[128,1024]{1,0:T(8,128)(2,1)S(1)} %get-tuple-element.44.refs_0_), channel_id=1, source_target_pairs={{0,8},{8,0},{16,24},{24,16},{1,9},{9,1},{17,25},{25,17},{2,10},{10... | collective-permute-start | bytes 786440 | tf_op jit(solution)/shard_map/ppermute | solution.py:19
  33.3 7.4 %collective-permute-start.12 = (bf16[128,1024]{1,0:T(8,128)(2,1)S(1)}, bf16[128,1024]{1,0:T(8,128)(2,1)S(1)}, u32[]{:S(2)}, u32[]{:S(2)}) collective-permute-start(bf16[128,1024]{1,0:T(8,128)(2,1)S(1)} %get-tuple-element.44.refs_0_), channel_id=1, source_target_pairs={{0,16},{8,24},{16,0},{24,8},{1,17},{9,25},{17,1},{25,9},{2,18},{10... | collective-permute-start | bytes 786440 | tf_op jit(solution)/shard_map/ppermute | solution.py:19
  34.7 4.9 %collective-permute-start.9 = (bf16[128,128]{1,0:T(8,128)(2,1)S(1)}, bf16[128,128]{1,0:T(8,128)(2,1)S(1)}, u32[]{:S(2)}, u32[]{:S(2)}) collective-permute-start(bf16[128,128]{1,0:T(8,128)(2,1)S(1)} %add_convert_fusion), channel_id=1, source_target_pairs={{0,4},{1,5},{2,6},{3,7},{4,0},{5,1},{6,2},{7,3},{8,12},{9,13},{10,... | collective-permute-start | bytes 98312 | tf_op jit(solution)/shard_map/ppermute | solution.py:19
  37.9 4.9 %collective-permute-start.15 = (bf16[128,1024]{1,0:T(8,128)(2,1)S(1)}, bf16[128,1024]{1,0:T(8,128)(2,1)S(1)}, u32[]{:S(2)}, u32[]{:S(2)}) collective-permute-start(bf16[128,1024]{1,0:T(8,128)(2,1)S(1)} %collective-permute-done.8.refs_3_), channel_id=1, source_target_pairs={{0,1},{1,0},{2,3},{3,2},{4,5},{5,4},{6,7},{7,6},{8,9},{9,8},{10,11... | collective-permute-start | bytes 786440 | tf_op jit(solution)/shard_map/ppermute | solution.py:19
  40.7 2.0 %collective-permute-start.13 = (bf16[128,1024]{1,0:T(8,128)(2,1)S(1)}, bf16[128,1024]{1,0:T(8,128)(2,1)S(1)}, u32[]{:S(2)}, u32[]{:S(2)}) collective-permute-start(bf16[128,1024]{1,0:T(8,128)(2,1)S(1)} %collective-permute-done.11.refs_1_), channel_id=1, source_target_pairs={{0,1},{1,0},{2,3},{3,2},{4,5},{5,4},{6,7},{7,6},{8,9},{9,8},{10,11... | collective-permute-start | bytes 786440 | tf_op jit(solution)/shard_map/ppermute | solution.py:19
  40.8 2.0 %collective-permute-start.14 = (bf16[128,1024]{1,0:T(8,128)(2,1)S(1)}, bf16[128,1024]{1,0:T(8,128)(2,1)S(1)}, u32[]{:S(2)}, u32[]{:S(2)}) collective-permute-start(bf16[128,1024]{1,0:T(8,128)(2,1)S(1)} %collective-permute-done.12.refs_2_), channel_id=1, source_target_pairs={{0,1},{1,0},{2,3},{3,2},{4,5},{5,4},{6,7},{7,6},{8,9},{9,8},{10,11... | collective-permute-start | bytes 786440 | tf_op jit(solution)/shard_map/ppermute | solution.py:19
  41.3 1.5 %collective-permute-start.10 = (bf16[256,128]{1,0:T(8,128)(2,1)S(1)}, bf16[256,128]{1,0:T(8,128)(2,1)S(1)}, u32[]{:S(2)}, u32[]{:S(2)}) collective-permute-start(bf16[256,128]{1,0:T(8,128)(2,1)S(1)} %get-tuple-element.43), channel_id=1, source_target_pairs={{0,1},{1,0},{2,3},{3,2},{4,5},{5,4},{6,7},{7,6},{8,9},{9,8},{10,11... | collective-permute-start | bytes 196616 | tf_op jit(solution)/shard_map/ppermute | solution.py:19
